TPU v7x, 32 devices: a whole 2x2x4 slice. The times are simulated.
32 devices in a mesh: dp: 2 (over y), band: 16 (over z, x, core).
Axes of the slice: x: 2, y: 2, z: 4, core: 2. Of those that a mesh axis runs over, the one named last changes fastest.
Arguments:
- grad_out: bfloat16 [2, 16, 128, 1024], P('dp', None, 'band'), may hold values from -6 to 6
- features: bfloat16 [2, 32, 128, 1024], P('dp', None, 'band'), may hold values from -6 to 6
- conv_weight: bfloat16 [3, 3, 16, 32], replicated, may hold values from -0.5 to 0.5
- block_weights: bfloat16 [1536, 128, 128], P('band'), may hold values from 0 to 0.049804688
- fine_tile: int32 [1536], P('band'), may hold values from 0 to 63
- coarse_tile: int32 [1536], P('band'), may hold values from 0 to 95, as said below
- owner_slot: int32 [96], replicated, may hold values from 0 to 95, as said below
- send_counts: int32 [16, 16], P('band'), may hold values from 0 to 12, as said below
Outputs:
- grad_features: bfloat16 [2, 32, 128, 1024], P('dp', None, 'band')
- conv_grad: float32 [3, 3, 16, 32], replicated
- coarse_grad: float32 [2, 96, 16, 128], P('dp', 'band')
Inputs may be any that keep to these rules, and one draw needn't show every extreme that they name: `send_counts`: row b names, for each owner, how many of band b's first blocks have coarse tiles that this owner holds; one owner gets exactly 12 from every band; a row sums to between 48 and 96, and to 96 in some band. `coarse_tile`: the live blocks of a band are ordered by owner as send_counts gives: those of owner 0 first, then those of owner 1, and so on. `owner_slot`: each value once; coarse tile t is held by band owner_slot[t] // 6 at place owner_slot[t] % 6.
All inputs are finite; a program needn't handle non-finite values.
Results may differ from a plain program's by a relative error of at most 0.005.
Values may be sent and summed in bfloat16 or wider, within the bound.
A program may use at most 64 MiB of HBM per device.

v0:
```python
import math

import jax
import jax.numpy as jnp
from jax import lax
from jax.sharding import PartitionSpec as P


def with_halo(block, sides, width):
    for axis, dim in sides:
        count = lax.axis_size(axis)
        forward = [(i, i + 1) for i in range(count - 1)]
        backward = [(target, source) for source, target in forward]
        low = lax.ppermute(
            lax.slice_in_dim(block, block.shape[dim] - width, None, axis=dim), axis, forward
        )
        high = lax.ppermute(lax.slice_in_dim(block, 0, width, axis=dim), axis, backward)
        block = jnp.concatenate([low, block, high], axis=dim)
    return block


def per_device(
    grad_out, features, conv_weight, block_weights, fine_tile, coarse_tile, owner_slot, send_counts
):
    bands = lax.axis_size("band")
    channels = grad_out.shape[1]
    row_count = grad_out.shape[2]
    col_count = grad_out.shape[3]
    tile_len = block_weights.shape[1]
    block_count = block_weights.shape[0]
    tiles_here = row_count * col_count // tile_len
    per_owner = owner_slot.shape[0] // bands
    tallies = send_counts[0]
    block_ids = jnp.arange(block_count, dtype=jnp.int32)
    in_use = block_ids < jnp.sum(tallies)
    cotangent = grad_out[0]
    tiles_local = cotangent.reshape(channels, tiles_here, tile_len)
    picked = jnp.take(tiles_local, fine_tile, axis=1)
    partial_value = jnp.einsum(
        "cbi,bij->bcj", picked, block_weights, preferred_element_type=jnp.float32
    )
    flat_terms = jnp.where(
        in_use[:, None], partial_value.reshape(block_count, channels * tile_len), 0.0
    )
    slot_of = jnp.take(owner_slot, coarse_tile)
    wanted = jnp.arange(per_owner * lax.axis_size("band"), dtype=jnp.int32)
    selector = ((slot_of[None, :] == wanted[:, None]) & in_use[None, :]).astype(jnp.float32)
    owned_sums = lax.psum_scatter(
        jnp.dot(
            selector,
            flat_terms,
            precision=lax.Precision.HIGHEST,
            preferred_element_type=jnp.float32,
        ),
        "band",
        scatter_dimension=0,
        tiled=True,
    )
    everyone = lax.all_gather(owned_sums, "band", axis=0, tiled=True)
    returned = jnp.take(everyone, slot_of, axis=0)
    returned = jnp.where(in_use[:, None], returned, 0.0).reshape(block_count, channels, tile_len)
    upper_part = returned.astype(jnp.bfloat16)
    lower_part = (returned - upper_part.astype(jnp.float32)).astype(jnp.bfloat16)
    spread = jnp.einsum(
        "bcj,bij->bci", upper_part, block_weights, preferred_element_type=jnp.float32
    )
    spread = spread + jnp.einsum(
        "bcj,bij->bci", lower_part, block_weights, preferred_element_type=jnp.float32
    )
    tile_pick = (
        (fine_tile[None, :] == jnp.arange(tiles_here, dtype=jnp.int32)[:, None]) & in_use[None, :]
    ).astype(jnp.float32)
    correction = jnp.dot(
        tile_pick,
        spread.reshape(block_count, -1),
        precision=lax.Precision.HIGHEST,
        preferred_element_type=jnp.float32,
    )
    correction = jnp.transpose(
        correction.reshape(tiles_here, channels, tile_len), (1, 0, 2)
    ).reshape(channels, row_count, col_count)
    grad_mid = (cotangent.astype(jnp.float32) - correction).astype(jnp.bfloat16)
    grad_rim = with_halo(grad_mid, (("band", 1),), 1)
    padded_mid = jnp.pad(grad_rim, ((0, 0), (0, 0), (1, 1)))
    inputs = features[0]
    feature_rim = with_halo(inputs, (("band", 1),), 1)
    padded_in = jnp.pad(feature_rim, ((0, 0), (0, 0), (1, 1)))
    total = jnp.zeros((inputs.shape[0], row_count, col_count), jnp.float32)
    kernel_rows = []
    for row_shift in range(3):
        kernel_cols = []
        for col_shift in range(3):
            window_mid = padded_mid[
                :,
                2 - row_shift : 2 - row_shift + row_count,
                2 - col_shift : 2 - col_shift + col_count,
            ]
            total = total + jnp.einsum(
                "ki,krq->irq",
                conv_weight[row_shift, col_shift],
                window_mid,
                preferred_element_type=jnp.float32,
            )
            window_in = padded_in[
                :, row_shift : row_shift + row_count, col_shift : col_shift + col_count
            ]
            kernel_cols.append(
                jnp.einsum("krq,irq->ki", grad_mid, window_in, preferred_element_type=jnp.float32)
            )
        kernel_rows.append(jnp.stack(kernel_cols))
    scaling = 1.0 / math.sqrt(lax.axis_size("dp") * bands * row_count * col_count)
    stacked = jnp.stack(kernel_rows) * scaling
    conv_grad = lax.psum(stacked, ("dp", "band"))
    grad_features = total.astype(jnp.bfloat16)[None]
    coarse_grad = owned_sums.reshape(1, per_owner, channels, tile_len)
    return (grad_features, conv_grad, coarse_grad)


def solution(mesh):
    placed = (
        P("dp", None, "band", None),
        P("dp", None, "band", None),
        P(),
        P("band", None, None),
        P("band"),
        P("band"),
        P(),
        P("band", None),
    )
    return jax.shard_map(
        per_device,
        mesh=mesh,
        in_specs=placed,
        out_specs=(P("dp", None, "band", None), P(), P("dp", "band", None, None)),
        check_vma=False,
    )
```

profile of v0, /device:TPU:0, one launch (start us, length us, event | category | flops | bytes accessed | tf_op | source)
XLA Modules:
  0.0 185.5 jit_solution(17977242629991526951)
XLA Ops:
  0.6 0.0 copy-start
  0.6 0.8 compare_and_fusion
  1.5 0.8 compare_select_fusion
  2.3 0.7 compare_select_fusion.2
  2.9 1.1 reshape_squeeze.3
  4.0 0.9 copy.25
  4.9 1.3 reduce_sum.9
  6.2 1.6 gather_fusion
  7.7 1.8 compare_and_fusion.1
  9.5 2.3 %gather_fusion.1 = bf16[96,16,128]{2,1,0:T(8,128)(2,1)} fusion(bf16[16,64,128]{2,0,1:T(8,128)(2,1)} %copy.25, s32[1024]{0:T(1024)S(1)} %pad_clamp_fusion.1), kind=kCustom, calls=%fused_computation.1 | custom fusion | bytes 786816 | tf_op jit(solution)/shard_map/jit(_take)/gather | solution.py:38
  11.9 2.0 %fusion.30 = f32[96,16,128]{2,1,0:T(8,128)S(1)} fusion(bf16[96,128,128]{2,1,0:T(8,128)(2,1)S(1)} %copy-done, bf16[96,16,128]{2,1,0:T(8,128)(2,1)} %gather_fusion.1, pred[96]{0:T(512)(128)(4,1)S(1)} %compare_and_fusion), kind=kOutput, calls=%fused_computation.62 | convolution fusion | flops 50528256 | bytes 4325472 | tf_op jit(solution)/shard_map/cbi,bij->bcj/dot_general | solution.py:39
  13.9 1.7 fusion.10
  15.6 41.9 %fusion = f32[8,2048]{1,0:T(8,128)S(1)} fusion(f32[96,2048]{1,0:T(8,128)} %fusion.10), kind=kCustom, calls=%all-reduce-scatter | all-reduce-scatter fusion | flops 262145 | bytes 852480
  57.5 1.3 collective-permute-start.6
  58.8 1.9 %collective-permute-start.5 = (f32[8,2048]{1,0:T(8,128)S(1)}, f32[8,2048]{1,0:T(8,128)}, u32[]{:S(2)}, u32[]{:S(2)}) collective-permute-start(f32[8,2048]{1,0:T(8,128)S(1)} %fusion), channel_id=1, source_target_pairs={{0,2},{1,3},{2,4},{3,5},{4,6},{5,7},{6,8},{7,9},{8,10},{9,11},{10,... | collective-permute-start | bytes 196616
  60.8 1.9 %collective-permute-start.4 = (f32[8,2048]{1,0:T(8,128)S(1)}, f32[8,2048]{1,0:T(8,128)}, u32[]{:S(2)}, u32[]{:S(2)}) collective-permute-start(f32[8,2048]{1,0:T(8,128)S(1)} %fusion), channel_id=1, source_target_pairs={{0,1},{1,2},{2,3},{3,4},{4,5},{5,6},{6,7},{7,8},{8,9},{9,10},{10,1... | collective-permute-start | bytes 196616
  62.7 0.6 slice.150
  63.3 1.9 %collective-permute-start.7 = (f32[6,2048]{1,0:T(8,128)}, f32[6,2048]{1,0:T(8,128)}, u32[]{:S(2)}, u32[]{:S(2)}) collective-permute-start(f32[6,2048]{1,0:T(8,128)} %slice.150), channel_id=1, source_target_pairs={{0,4},{1,5},{2,6},{3,7},{4,8},{5,9},{6,10},{7,11},{8,12},{9,13},{1... | collective-permute-start | bytes 147464
  65.2 1.3 copy.56
  66.5 0.8 copy-done.1
  67.3 0.7 fusion.88
  68.0 1.9 %collective-permute-start.2 = (bf16[32,1,1024]{2,0,1:T(8,128)(2,1)}, bf16[32,1,1024]{2,0,1:T(8,128)(2,1)}, u32[]{:S(2)}, u32[]{:S(2)}) collective-permute-start(bf16[32,1,1024]{2,0,1:T(8,128)(2,1)} %get-tuple-element.14), channel_id=1, source_target_pairs={{0,1},{1,2},{2,3},{3,4},{4,5},{5,6},{6,7},{7,8},{8,9},{9,10},{10,1... | collective-permute-start | bytes 196616 | tf_op jit(solution)/shard_map/ppermute | solution.py:14
  69.9 0.6 dynamic-slice.4
  71.2 1.3 collective-permute-start.3
  72.5 7.8 %concatenate.24 = f32[38,2048]{1,0:T(8,128)} concatenate(f32[6,2048]{1,0:T(8,128)} %collective-permute-done.7, f32[8,2048]{1,0:T(8,128)S(1)} %collective-permute-done.6, f32[8,2048]{1,0:T(8,128)} %collective-permute-done.5, f32[8,2048]{1,0:T(8,128)} %collective-permute-done.4, f32[8,2048]{1,0:T(8,128)S(1)} %fusion), dimensions={0} | concatenate | bytes 622592
  80.3 0.9 dynamic-slice_bitcast_fusion
  81.2 24.4 %all-gather = f32[16,6,2048]{2,1,0:T(8,128)} all-gather(f32[1,6,2048]{2,1,0:T(8,128)S(1)} %get-tuple-element.17), channel_id=1, replica_groups=mesh['dp'=2,'band'=16] {'band'}, dimensions={0}, use_global_device_ids=true | all-gather | bytes 835584 | tf_op jit(solution)/shard_map/all_gather | solution.py:59
  105.6 2.3 %reshape.101 = f32[96,2048]{1,0:T(8,128)} reshape(f32[16,6,2048]{2,1,0:T(8,128)} %all-gather) | data formatting | bytes 1572864
  107.8 3.2 %gather_fusion.2 = f32[96,2048]{1,0:T(8,128)} fusion(f32[96,2048]{1,0:T(8,128)} %reshape.101, s32[1024]{0:T(1024)S(1)} %pad_clamp_fusion), kind=kCustom, calls=%fused_computation.2 | custom fusion | bytes 1573248 | tf_op jit(solution)/shard_map/jit(_take)/gather | solution.py:60
  111.1 1.3 copy.33
  112.3 0.3 subtract_convert_fusion
  112.6 0.3 fusion.17
  112.9 1.7 fusion.90
  114.6 1.8 convolution_add_fusion.6
  116.4 1.6 subtract_convert_fusion.1
  118.0 1.9 %reshape.70 = f32[16,8,1024]{2,1,0:T(8,128)} reshape(f32[16,64,128]{2,1,0:T(8,128)} %get-tuple-element.21) | data formatting | bytes 1048576 | tf_op jit(solution)/shard_map/reshape | solution.py:81
  119.9 1.6 fusion.26
  121.5 1.4 fusion.15
  122.9 0.2 convolution_bitcast_fusion.3
  123.2 0.3 convolution_bitcast_fusion.4
  123.5 0.7 convolution_bitcast_fusion.5
  124.2 0.3 convolution_bitcast_fusion.6
  124.5 0.3 convolution_bitcast_fusion.7
  124.8 0.3 convolution_bitcast_fusion.9
  125.1 0.3 convolution_bitcast_fusion.1
  125.4 0.6 fusion.89
  126.1 2.9 %collective-permute-start = (bf16[16,1,1024]{2,0,1:T(8,128)(2,1)}, bf16[16,1,1024]{2,0,1:T(8,128)(2,1)}, u32[]{:S(2)}, u32[]{:S(2)}) collective-permute-start(bf16[16,1,1024]{2,0,1:T(8,128)(2,1)} %get-tuple-element.18), channel_id=1, source_target_pairs={{0,1},{1,2},{2,3},{3,4},{4,5},{5,6},{6,7},{7,8},{8,9},{9,10},{10,1... | collective-permute-start | bytes 98312 | tf_op jit(solution)/shard_map/ppermute | solution.py:14
  128.9 1.3 collective-permute-start.1
  130.2 1.1 convolution_bitcast_fusion.2
  131.3 1.1 convolution_bitcast_fusion.8
  132.5 0.6 copy.57
  133.1 1.8 convert_element_type.43
  134.9 42.2 %psum.7 = f32[3,3,16,32]{3,2,1,0:T(8,128)} all-reduce(f32[3,3,16,32]{3,2,1,0:T(8,128)S(1)} %maximum_multiply_fusion), channel_id=1, replica_groups=mesh['dp'=2,'band'=16] {'dp','band'}, use_global_device_ids=true, to_apply=%region_2.3 | all-reduce | flops 4608 | bytes 36864 | tf_op jit(solution)/shard_map/psum | solution.py:113
  177.1 0.9 fusion.37
  178.0 1.0 fusion.46
  179.0 1.1 fusion.38
  180.2 1.1 convolution_add_fusion.5
  181.3 0.3 convolution_add_fusion.4
  181.6 0.4 convolution_add_fusion.3
  182.0 0.4 convolution_add_fusion.2
  182.4 0.4 convolution_add_fusion.1
  182.8 1.1 fusion.42
  183.9 0.5 fusion.5
  184.4 1.1 copy.30
  (32 shorter events, 0.1 us)
Async XLA Ops:
  0.6 11.3 %copy-start = (bf16[96,128,128]{2,1,0:T(8,128)(2,1)S(1)}, bf16[96,128,128]{2,1,0:T(8,128)(2,1)}, u32[]{:S(2)}) copy-start(bf16[96,128,128]{2,1,0:T(8,128)(2,1)} %param.11) | copy-start | bytes 9437188
  11.9 58.0 %copy-start.8 = (u32[32]{0:T(128)S(1)}, u32[32]{0:T(128)}, u32[]{:S(2)}) copy-start(u32[32]{0:T(128)} %constant.60) | copy-start | bytes 388
  57.5 14.9 %collective-permute-start.6 = (f32[8,2048]{1,0:T(8,128)S(1)}, f32[8,2048]{1,0:T(8,128)S(1)}, u32[]{:S(2)}, u32[]{:S(2)}) collective-permute-start(f32[8,2048]{1,0:T(8,128)S(1)} %fusion), channel_id=1, source_target_pairs={{0,3},{1,4},{2,5},{3,6},{4,7},{5,8},{6,9},{7,10},{8,11},{9,12},{10... | collective-permute-start | bytes 196616
  58.8 13.7 %collective-permute-start.5 = (f32[8,2048]{1,0:T(8,128)S(1)}, f32[8,2048]{1,0:T(8,128)}, u32[]{:S(2)}, u32[]{:S(2)}) collective-permute-start(f32[8,2048]{1,0:T(8,128)S(1)} %fusion), channel_id=1, source_target_pairs={{0,2},{1,3},{2,4},{3,5},{4,6},{5,7},{6,8},{7,9},{8,10},{9,11},{10,... | collective-permute-start | bytes 196616
  60.8 11.7 %collective-permute-start.4 = (f32[8,2048]{1,0:T(8,128)S(1)}, f32[8,2048]{1,0:T(8,128)}, u32[]{:S(2)}, u32[]{:S(2)}) collective-permute-start(f32[8,2048]{1,0:T(8,128)S(1)} %fusion), channel_id=1, source_target_pairs={{0,1},{1,2},{2,3},{3,4},{4,5},{5,6},{6,7},{7,8},{8,9},{9,10},{10,1... | collective-permute-start | bytes 196616
  63.3 7.9 %collective-permute-start.7 = (f32[6,2048]{1,0:T(8,128)}, f32[6,2048]{1,0:T(8,128)}, u32[]{:S(2)}, u32[]{:S(2)}) collective-permute-start(f32[6,2048]{1,0:T(8,128)} %slice.150), channel_id=1, source_target_pairs={{0,4},{1,5},{2,6},{3,7},{4,8},{5,9},{6,10},{7,11},{8,12},{9,13},{1... | collective-permute-start | bytes 147464
  66.5 0.8 copy-start.1
  68.0 53.5 %collective-permute-start.2 = (bf16[32,1,1024]{2,0,1:T(8,128)(2,1)}, bf16[32,1,1024]{2,0,1:T(8,128)(2,1)}, u32[]{:S(2)}, u32[]{:S(2)}) collective-permute-start(bf16[32,1,1024]{2,0,1:T(8,128)(2,1)} %get-tuple-element.14), channel_id=1, source_target_pairs={{0,1},{1,2},{2,3},{3,4},{4,5},{5,6},{6,7},{7,8},{8,9},{9,10},{10,1... | collective-permute-start | bytes 196616 | tf_op jit(solution)/shard_map/ppermute | solution.py:14
  71.2 50.4 %collective-permute-start.3 = (bf16[32,1,1024]{2,0,1:T(8,128)(2,1)}, bf16[32,1,1024]{2,0,1:T(8,128)(2,1)}, u32[]{:S(2)}, u32[]{:S(2)}) collective-permute-start(bf16[32,1,1024]{2,0,1:T(8,128)(2,1)} %get-tuple-element.15), channel_id=1, source_target_pairs={{1,0},{2,1},{3,2},{4,3},{5,4},{6,5},{7,6},{8,7},{9,8},{10,9},{11,1... | collective-permute-start | bytes 196616 | tf_op jit(solution)/shard_map/ppermute | solution.py:17
  107.8 4.5 %copy-start.6 = (pred[96]{0:T(512)(128)(4,1)S(1)}, pred[96]{0:T(512)(128)(4,1)}, u32[]{:S(2)}) copy-start(pred[96]{0:T(512)(128)(4,1)} %get-tuple-element.12) | copy-start | bytes 292
  114.6 1.8 copy-start.7
  119.9 3.6 %copy-start.4 = (bf16[1,32,8,1024]{3,2,1,0:T(8,128)(2,1)S(1)}, bf16[1,32,8,1024]{3,2,1,0:T(8,128)(2,1)}, u32[]{:S(2)}) copy-start(bf16[1,32,8,1024]{3,2,1,0:T(8,128)(2,1)} %param.9) | copy-start | bytes 1572868
  122.9 7.3 %copy-start.2 = (bf16[1,32,8,1024]{3,1,2,0:T(8,128)(2,1)S(1)}, bf16[1,32,8,1024]{3,1,2,0:T(8,128)(2,1)}, u32[]{:S(2)}) copy-start(bf16[1,32,8,1024]{3,1,2,0:T(8,128)(2,1)} %copy-done.1) | copy-start | bytes 1572868
  126.1 51.0 %collective-permute-start = (bf16[16,1,1024]{2,0,1:T(8,128)(2,1)}, bf16[16,1,1024]{2,0,1:T(8,128)(2,1)}, u32[]{:S(2)}, u32[]{:S(2)}) collective-permute-start(bf16[16,1,1024]{2,0,1:T(8,128)(2,1)} %get-tuple-element.18), channel_id=1, source_target_pairs={{0,1},{1,2},{2,3},{3,4},{4,5},{5,6},{6,7},{7,8},{8,9},{9,10},{10,1... | collective-permute-start | bytes 98312 | tf_op jit(solution)/shard_map/ppermute | solution.py:14
  128.9 48.2 %collective-permute-start.1 = (bf16[16,1,1024]{2,0,1:T(8,128)(2,1)}, bf16[16,1,1024]{2,0,1:T(8,128)(2,1)}, u32[]{:S(2)}, u32[]{:S(2)}) collective-permute-start(bf16[16,1,1024]{2,0,1:T(8,128)(2,1)} %get-tuple-element.19), channel_id=1, source_target_pairs={{1,0},{2,1},{3,2},{4,3},{5,4},{6,5},{7,6},{8,7},{9,8},{10,9},{11,1... | collective-permute-start | bytes 98312 | tf_op jit(solution)/shard_map/ppermute | solution.py:17
  133.1 48.2 %copy-start.5 = (bf16[3,3,16,32]{3,2,1,0:T(8,128)(2,1)S(1)}, bf16[3,3,16,32]{3,2,1,0:T(8,128)(2,1)}, u32[]{:S(2)}) copy-start(bf16[3,3,16,32]{3,2,1,0:T(8,128)(2,1)} %param.10) | copy-start | bytes 27652
  180.1 1.9 %copy-start.3 = (bf16[16,8,1024]{2,1,0:T(8,128)(2,1)S(1)}, bf16[16,8,1024]{2,1,0:T(8,128)(2,1)}, u32[]{:S(2)}) copy-start(bf16[16,8,1024]{2,1,0:T(8,128)(2,1)} %convert_element_type.43) | copy-start | bytes 786436
where the time goes:
time: 187 us; the launch traced here: 185 us
  blocking collectives  109 us (58%)
  local copies, waits for them, and re-layouts  31.4 us (17%)
  matrix products  19.7 us (11%)
  starting transfers between devices  14.4 us (8%)
  other arithmetic  9.9 us (5%)
    psum x1, blocking collectives, per_device(): conv_grad = lax.psum(stacked, ('dp', 'band'))  42.2 us
    unnamed x1, blocking collectives  41.9 us
    all_gather x1, blocking collectives, per_device(): everyone = lax.all_gather(owned_sums, 'band', axis=0, tiled=True)  24.4 us
    unnamed x27, local copies, waits for them, and re-layouts  17.3 us
    unnamed x4, starting transfers between devices  7.03 us
    dot_general x9, matrix products, per_device(): jnp.einsum('ki,krq->irq', conv_weight[row_shift, col_shift], window_mid,...  6.29 us
    ppermute x2, starting transfers between devices, with_halo(): lax.ppermute(lax.slice_in_dim(block, block.shape[dim] - width, None, axis...  4.76 us
    dot_general x9, matrix products, per_device(): jnp.einsum('krq,irq->ki', grad_mid, window_in, preferred_element_type=jnp...  4.65 us
  transfers between devices with their start and end apart: 8, of which 0 were waited for; matrix products, arithmetic and copies ran while one was open for 17% of the time, Pallas kernels for 0%

commit v1 on v0

v1 whole, which is shorter than its diff:
```python
import functools
import math

import jax
import jax.numpy as jnp
from jax import lax
from jax.experimental import pallas as pl
from jax.experimental.pallas import tpu as pltpu
from jax.sharding import PartitionSpec as P

F32 = jnp.float32
BF16 = jnp.bfloat16
MESH = pl.DeviceIdType.MESH
NT = (((1,), (1,)), ((), ()))


def split_bf16(value):
    high = value.astype(BF16)
    low = (value - high.astype(F32)).astype(BF16)
    return high, low


def kernel(
    dims,
    ft_s,
    ct_s,
    os_s,
    ft_v,
    ct_v,
    os_v,
    sc_v,
    go,
    feat,
    cw,
    weights,
    gf_out,
    cg_out,
    co_out,
    stage,
    tiles,
    terms,
    sums,
    tx1,
    rx1,
    tx2,
    rx2,
    back,
    corr,
    comb,
    featr,
    edges,
    halo,
    ar1,
    ar2,
    ar3,
    s1s,
    s1r,
    s2s,
    s2r,
    gos,
    gis,
    grs,
    hs,
    hr,
    a1s,
    a1r,
    a2s,
    a2r,
    a3s,
    a3r,
):
    n_dp, bands, n1, n2, channels, cin, rows, cols, tl, nb, per, ct_all, scaling = dims
    cblocks = cols // tl
    n_tiles = rows * cblocks
    group = n2 * per
    me = lax.axis_index("band")
    my_dp = lax.axis_index("dp")
    my_o = me // n1
    my_i = me % n1

    barrier = pltpu.get_barrier_semaphore()

    def inner(i):
        return {"band": my_o * n1 + i}

    def outer(z):
        return {"band": z * n1 + my_i}

    def greet(device):
        pl.semaphore_signal(barrier, inc=1, device_id=device, device_id_type=MESH)

    for d in range(1, n1):
        greet(inner((my_i + d) % n1))
    for e in range(1, n2):
        greet(outer((my_o + e) % n2))
    for f in range(1, n_dp):
        greet({"dp": (my_dp + f) % n_dp})

    @pl.when(me > 0)
    def _():
        greet({"band": me - 1})

    @pl.when(me < bands - 1)
    def _():
        greet({"band": me + 1})

    for b in range(cblocks):
        part = go[:, :, b * tl : (b + 1) * tl].astype(F32)
        stage[b, 0 : channels * rows, :] = part.reshape(channels * rows, tl)
        for r in range(rows):
            line = stage[b, pl.ds(r, channels, stride=rows), :]
            tiles[r * cblocks + b] = line.astype(BF16)

    step = 8

    def forward(t, carry):
        for a in range(step):
            k = t * step + a
            product = jnp.dot(tiles[ft_s[k]], weights[k], preferred_element_type=F32)
            terms[pl.ds(pl.multiple_of(k * channels, channels), channels), :] = product
        return carry

    lax.fori_loop(0, nb // step, forward, 0)

    def owner_parts(slot):
        owner = lax.shift_right_logical(slot * (65536 // per + 1), 16)
        place = slot - owner * per
        z = lax.shift_right_logical(owner, n1.bit_length() - 1)
        i = owner & (n1 - 1)
        return (i * n2 + z) * per + place

    live = jnp.sum(sc_v[...], axis=1, keepdims=True)
    in_use = lax.broadcasted_iota(jnp.int32, (1, nb), 1) < live
    eye = lax.broadcasted_iota(jnp.int32, (ct_all, ct_all), 0) == lax.broadcasted_iota(
        jnp.int32, (ct_all, ct_all), 1
    )
    row_of = owner_parts(os_v[...])
    column = jnp.sum(jnp.where(eye, row_of, 0), axis=1, keepdims=True)
    match = lax.broadcasted_iota(jnp.int32, (ct_all, nb), 0) == ct_v[...]
    row_of_block = jnp.sum(jnp.where(match, column, 0), axis=0, keepdims=True)
    row_of_block = jnp.where(in_use, row_of_block, -1)
    select = (lax.broadcasted_iota(jnp.int32, (ct_all, nb), 0) == row_of_block).astype(F32)
    select = jnp.concatenate([select.astype(BF16)] * 2, axis=1)
    fine = jnp.where(in_use, ft_v[...], -1)
    pick = (lax.broadcasted_iota(jnp.int32, (n_tiles, nb), 0) == fine).astype(F32)
    pick = jnp.concatenate([pick.astype(BF16)] * 2, axis=1)

    def gather_sum(chooser, target, count):
        for c in range(0, channels, 2):
            parts = [terms[pl.ds(c + a, nb, stride=channels), :] for a in range(2)]
            high, low = split_bf16(jnp.concatenate(parts, axis=1))
            both = jnp.concatenate([high, low], axis=0)
            total = jnp.dot(chooser, both, preferred_element_type=F32)
            for a in range(2):
                target[pl.ds(c + a, count, stride=channels), :] = total[:, a * tl : (a + 1) * tl]

    gather_sum(select, sums, ct_all)
    tx1[...] = sums[...].astype(BF16).reshape(ct_all, channels, tl)

    peers = (n1 - 1) + (n2 - 1) + (n_dp - 1)
    peers = peers + jnp.minimum(me, 1) + jnp.minimum(bands - 1 - me, 1)
    pl.semaphore_wait(barrier, peers)

    def remote(src, dst, send, recv, device):
        return pltpu.make_async_remote_copy(
            src_ref=src,
            dst_ref=dst,
            send_sem=send,
            recv_sem=recv,
            device_id=device,
            device_id_type=MESH,
        )

    first = []
    for d in range(1, n1):
        to = (my_i + d) % n1
        copy = remote(
            tx1.at[pl.ds(to * group, group)], rx1.at[d - 1], s1s.at[d - 1], s1r.at[d - 1], inner(to)
        )
        copy.start()
        first.append(copy)

    for b in range(cblocks):
        part = feat[:, :, b * tl : (b + 1) * tl].astype(F32)
        stage[b] = part.reshape(cin * rows, tl)
        for r in range(rows):
            line = stage[b, pl.ds(r, cin, stride=rows), :]
            featr[r, :, b * tl : (b + 1) * tl] = line.astype(BF16)
    slab = 3 * channels
    kernel_rows = jnp.concatenate([cw[(2 - p) * slab : (3 - p) * slab, :] for p in range(3)], axis=0)
    kernel_t = kernel_rows.astype(F32).T.astype(BF16)

    for copy in first:
        copy.wait()

    size = per * channels

    def inner_sum(z):
        own = sums[pl.ds(pl.multiple_of((my_i * group + z * per) * channels, size), size), :]
        for d in range(n1 - 1):
            own = own + rx1[d, pl.ds(z * per, per)].astype(F32).reshape(size, tl)
        return own

    second = []
    for e in range(1, n2):
        to = (my_o + e) % n2
        tx2[e - 1] = inner_sum(to).astype(BF16).reshape(per, channels, tl)
        copy = remote(tx2.at[e - 1], rx2.at[e - 1], s2s.at[e - 1], s2r.at[e - 1], outer(to))
        copy.start()
        second.append(copy)
    owned = inner_sum(my_o)
    for e in range(1, n2):
        second[e - 1].wait()
        owned = owned + rx2[e - 1].astype(F32).reshape(size, tl)

    def place(i, z):
        return back.at[pl.ds((i * n2 + z) * per, per)]

    back[pl.ds((my_i * n2 + my_o) * per, per)] = owned.astype(BF16).reshape(per, channels, tl)

    sent = []

    def pass_on(z, e):
        here = place(my_i, z)
        for d in range(1, n1):
            copy = remote(
                here, here, gis.at[d - 1, e], grs.at[my_i, z], inner((my_i + d) % n1)
            )
            copy.start()
            sent.append(copy)

    mine = place(my_i, my_o)
    for e in range(1, n2):
        copy = remote(mine, mine, gos.at[e - 1], grs.at[my_i, my_o], outer((my_o + e) % n2))
        copy.start()
        sent.append(copy)
    pass_on(my_o, 0)
    co_out[...] = owned.reshape(per, channels, tl)
    for e in range(1, n2):
        z = (my_o + n2 - e) % n2
        here = place(my_i, z)
        remote(here, here, gos.at[e - 1], grs.at[my_i, z], outer(z)).wait_recv()
        pass_on(z, e)
    for d in range(1, n1):
        i = (my_i + d) % n1
        for e in range(n2):
            z = (my_o + n2 - e) % n2
            here = place(i, z)
            remote(here, here, gis.at[d - 1, e], grs.at[i, z], inner(i)).wait_recv()
    for copy in sent:
        copy.wait_send()

    def row_index(slot):
        owner = slot // per
        return ((owner % n1) * n2 + owner // n1) * per + slot % per

    def backward(t, carry):
        for a in range(step):
            k = t * step + a
            value = back[row_index(os_s[ct_s[k]])]
            product = lax.dot_general(value, weights[k], NT, preferred_element_type=F32)
            terms[pl.ds(pl.multiple_of(k * channels, channels), channels), :] = product
        return carry

    lax.fori_loop(0, nb // step, backward, 0)
    gather_sum(pick, corr, n_tiles)

    col = lax.broadcasted_iota(jnp.int32, (channels, cols), 1)

    def mid_row(r):
        parts = []
        for b in range(cblocks):
            g = r * cblocks + b
            parts.append(tiles[g].astype(F32) - corr[g * channels : (g + 1) * channels, :])
        return jnp.concatenate(parts, axis=1).astype(BF16)

    def put_row(p, line):
        wide = line.astype(F32)
        later = jnp.where(col == cols - 1, 0.0, pltpu.roll(wide, cols - 1, 1))
        earlier = jnp.where(col == 0, 0.0, pltpu.roll(wide, 1, 1))
        comb[p * slab : p * slab + channels, :] = later.astype(BF16)
        comb[p * slab + channels : p * slab + 2 * channels, :] = line
        comb[p * slab + 2 * channels : (p + 1) * slab, :] = earlier.astype(BF16)

    top, bottom = mid_row(0), mid_row(rows - 1)
    edges[0] = top
    edges[1] = bottom
    up = remote(edges.at[0], halo.at[1], hs.at[0], hr.at[1], {"band": jnp.maximum(me - 1, 0)})
    down = remote(
        edges.at[1], halo.at[0], hs.at[1], hr.at[0], {"band": jnp.minimum(me + 1, bands - 1)}
    )

    @pl.when(me > 0)
    def _():
        up.start()

    @pl.when(me < bands - 1)
    def _():
        down.start()

    put_row(1, top)
    put_row(rows, bottom)
    for r in range(1, rows - 1):
        put_row(r + 1, mid_row(r))

    def conv_row(r, total):
        window = comb[r * slab : (r + 3) * slab, :]
        result = jnp.dot(kernel_t, window, preferred_element_type=F32)
        for b in range(cblocks):
            stage[b, pl.ds(r, cin, stride=rows), :] = result[:, b * tl : (b + 1) * tl]
        return total + lax.dot_general(window, featr[r], NT, preferred_element_type=F32)

    total = jnp.zeros((3 * slab, cin), F32)
    for r in range(1, rows - 1):
        total = conv_row(r, total)

    @pl.when(me > 0)
    def _():
        down.wait_recv()
        put_row(0, halo[0])

    @pl.when(me == 0)
    def _():
        comb[0:slab, :] = jnp.zeros((slab, cols), BF16)

    @pl.when(me < bands - 1)
    def _():
        up.wait_recv()
        put_row(rows + 1, halo[1])

    @pl.when(me == bands - 1)
    def _():
        comb[(rows + 1) * slab : (rows + 2) * slab, :] = jnp.zeros((slab, cols), BF16)

    total = conv_row(0, total)
    total = conv_row(rows - 1, total)

    total = total * scaling
    packs = 128 // cin
    lines = ar1.shape[1]
    full = jnp.concatenate([total, jnp.zeros((packs * lines - 3 * slab, cin), F32)], axis=0)
    packed = jnp.concatenate([full[a * lines : (a + 1) * lines] for a in range(packs)], axis=1)

    def exchange(value, buf, send, recv, count, index, device):
        buf[index] = value
        copies = []
        for d in range(1, count):
            copy = remote(
                buf.at[index],
                buf.at[index],
                send.at[d - 1],
                recv.at[index],
                device((index + d) % count),
            )
            copy.start()
            copies.append(copy)

        def finish():
            for d in range(1, count):
                source = (index + d) % count
                remote(
                    buf.at[source], buf.at[source], send.at[d - 1], recv.at[source], device(source)
                ).wait_recv()
            for copy in copies:
                copy.wait_send()
            result = buf[0]
            for m in range(1, count):
                result = result + buf[m]
            return result

        return finish

    finish = exchange(packed, ar1, a1s, a1r, n1, my_i, inner)
    for b in range(cblocks):
        part = stage[b].reshape(cin, rows, tl)
        gf_out[:, :, b * tl : (b + 1) * tl] = part.astype(BF16)
    packed = finish()
    packed = exchange(packed, ar2, a2s, a2r, n2, my_o, outer)()
    packed = exchange(packed, ar3, a3s, a3r, n_dp, my_dp, lambda y: {"dp": y})()
    for u in range(3):
        for s in range((2 - u) * slab, (3 - u) * slab, 8):
            a, b = s // lines, s % lines
            at = u * slab + s - (2 - u) * slab
            cg_out[at : at + 8, :] = packed[b : b + 8, a * cin : (a + 1) * cin]

    @pl.when(me > 0)
    def _():
        up.wait_send()

    @pl.when(me < bands - 1)
    def _():
        down.wait_send()


def per_device(
    n_dp,
    bands,
    grad_out,
    features,
    conv_weight,
    block_weights,
    fine_tile,
    coarse_tile,
    owner_slot,
    send_counts,
):
    channels, rows, cols = grad_out.shape[1:]
    cin = features.shape[1]
    nb, tl = block_weights.shape[:2]
    ct_all = owner_slot.shape[0]
    per = ct_all // bands
    n1 = 4
    n2 = bands // n1
    n_tiles = rows * cols // tl
    scaling = 1.0 / math.sqrt(n_dp * bands * rows * cols)
    dims = (n_dp, bands, n1, n2, channels, cin, rows, cols, tl, nb, per, ct_all, scaling)
    slab = 3 * channels
    packs = 128 // cin
    lines = -(-3 * slab // (packs * 8)) * 8
    group = n2 * per
    dma = pltpu.SemaphoreType.DMA
    vmem = pl.BlockSpec(memory_space=pltpu.VMEM)
    smem = pl.BlockSpec(memory_space=pltpu.SMEM)
    gf, cg, co = pl.pallas_call(
        functools.partial(kernel, dims),
        out_shape=(
            jax.ShapeDtypeStruct((cin, rows, cols), BF16),
            jax.ShapeDtypeStruct((3 * slab, cin), F32),
            jax.ShapeDtypeStruct((per, channels, tl), F32),
        ),
        in_specs=[smem] * 3 + [vmem] * 8,
        out_specs=(vmem, vmem, vmem),
        scratch_shapes=[
            pltpu.VMEM((cols // tl, cin * rows, tl), F32),
            pltpu.VMEM((n_tiles, channels, tl), BF16),
            pltpu.VMEM((nb * channels, tl), F32),
            pltpu.VMEM((ct_all * channels, tl), F32),
            pltpu.VMEM((ct_all, channels, tl), BF16),
            pltpu.VMEM((n1 - 1, group, channels, tl), BF16),
            pltpu.VMEM((n2 - 1, per, channels, tl), BF16),
            pltpu.VMEM((n2 - 1, per, channels, tl), BF16),
            pltpu.VMEM((ct_all, channels, tl), BF16),
            pltpu.VMEM((n_tiles * channels, tl), F32),
            pltpu.VMEM(((rows + 2) * slab, cols), BF16),
            pltpu.VMEM((rows, cin, cols), BF16),
            pltpu.VMEM((2, channels, cols), BF16),
            pltpu.VMEM((2, channels, cols), BF16),
            pltpu.VMEM((n1, lines, 128), F32),
            pltpu.VMEM((n2, lines, 128), F32),
            pltpu.VMEM((n_dp, lines, 128), F32),
            dma((n1 - 1,)),
            dma((n1 - 1,)),
            dma((n2 - 1,)),
            dma((n2 - 1,)),
            dma((n2 - 1,)),
            dma((n1 - 1, n2)),
            dma((n1, n2)),
            dma((2,)),
            dma((2,)),
            dma((n1 - 1,)),
            dma((n1,)),
            dma((n2 - 1,)),
            dma((n2,)),
            dma((n_dp - 1,)),
            dma((n_dp,)),
        ],
        compiler_params=pltpu.CompilerParams(
            collective_id=0, has_side_effects=True, vmem_limit_bytes=48 * 1024 * 1024
        ),
    )(
        fine_tile,
        coarse_tile,
        owner_slot,
        fine_tile.reshape(1, nb),
        coarse_tile.reshape(1, nb),
        owner_slot.reshape(1, ct_all),
        send_counts,
        grad_out.reshape(channels, rows, cols),
        features.reshape(cin, rows, cols),
        conv_weight.reshape(3 * slab, cin),
        block_weights,
    )
    return gf[None], cg.reshape(3, 3, channels, cin), co[None]


def solution(mesh):
    placed = (
        P("dp", None, "band", None),
        P("dp", None, "band", None),
        P(),
        P("band", None, None),
        P("band"),
        P("band"),
        P(),
        P("band", None),
    )
    return jax.shard_map(
        functools.partial(per_device, mesh.shape["dp"], mesh.shape["band"]),
        mesh=mesh,
        in_specs=placed,
        out_specs=(P("dp", None, "band", None), P(), P("dp", "band", None, None)),
        check_vma=False,
    )
```

time: 187 us -> 51.2 us (0.27)
  blocking collectives: 109 us -> 0 us
  Pallas kernels: 0 us -> 40.9 us
  local copies, waits for them, and re-layouts: 31.4 us -> 9.31 us
  matrix products: 19.7 us -> 0 us
  starting transfers between devices: 14.4 us -> 0 us
  other arithmetic: 9.9 us -> 0 us
    psum x1 -> x0, blocking collectives: 42.2 us -> none  [per_device(): conv_grad = lax.psum(stacked, ('dp', 'band'))]
    unnamed x1 -> x0, blocking collectives: 41.9 us -> none
    pallas_call x0 -> x1, Pallas kernels: none -> 40.9 us  [per_device(): pl.pallas_call(functools.partial(kernel, dims), out_shape=(jax.ShapeDtype...]
    all_gather x1 -> x0, blocking collectives: 24.4 us -> none  [per_device(): everyone = lax.all_gather(owned_sums, 'band', axis=0, tiled=True)]
    dot_general x23 -> x0, matrix products: 19.7 us -> none  [the longest x9 6.29 us: per_device(): jnp.einsum('ki,krq->irq', conv_weight[row_shift, col_shift], window_mid,...]
    unnamed x27 -> x19, local copies, waits for them, and re-layouts: 17.3 us -> 9.31 us
    ppermute x4 -> x0, starting transfers between devices: 7.33 us -> none  [the longest x2 4.76 us: with_halo(): lax.ppermute(lax.slice_in_dim(block, block.shape[dim] - width, None, axis...]
    gather x3 -> x0, local copies, waits for them, and re-layouts: 7.15 us -> none  [the longest x1 3.22 us: per_device(): returned = jnp.take(everyone, slot_of, axis=0)]
  transfers between devices with their start and end apart: 8 -> 0, of which waited for: 0 -> 0; matrix products, arithmetic and copies ran while one was open for 17% -> 0% of each run, Pallas kernels for 0% -> 0%
where the time goes in v1:
time: 51.2 us; the launch traced here: 50.9 us
  Pallas kernels  40.9 us (80%)
  local copies, waits for them, and re-layouts  9.31 us (18%)
  between operations  0.66 us (1%)
    pallas_call x1, Pallas kernels, per_device(): pl.pallas_call(functools.partial(kernel, dims), out_shape=(jax.ShapeDtype...  40.9 us
    unnamed x19, local copies, waits for them, and re-layouts  9.31 us

profile of v1, /device:TPU:0, one launch (start us, length us, event | category | flops | bytes accessed | tf_op | source)
XLA Modules:
  0.0 50.9 jit_solution(17715666202260301966)
XLA Ops:
  0.6 0.0 copy-start
  0.6 1.9 %copy-done = bf16[96,128,128]{2,1,0:T(8,128)(2,1)S(1)} copy-done((bf16[96,128,128]{2,1,0:T(8,128)(2,1)S(1)}, bf16[96,128,128]{2,1,0:T(8,128)(2,1)}, u32[]{:S(2)}) %copy-start) | copy-done | bytes 3145752
  2.5 0.0 copy-start.1
  2.5 1.0 %copy-done.1 = bf16[1,32,8,1024]{3,2,1,0:T(8,128)(2,1)S(1)} copy-done((bf16[1,32,8,1024]{3,2,1,0:T(8,128)(2,1)S(1)}, bf16[1,32,8,1024]{3,2,1,0:T(8,128)(2,1)}, u32[]{:S(2)}) %copy-start.1) | copy-done | bytes 524312
  3.6 0.0 copy-start.2
  3.6 0.9 %copy-done.2 = bf16[1,16,8,1024]{3,2,1,0:T(8,128)(2,1)S(1)} copy-done((bf16[1,16,8,1024]{3,2,1,0:T(8,128)(2,1)S(1)}, bf16[1,16,8,1024]{3,2,1,0:T(8,128)(2,1)}, u32[]{:S(2)}) %copy-start.2) | copy-done | bytes 262168
  4.5 0.0 copy-start.3
  4.5 0.8 %copy-done.3 = bf16[3,3,16,32]{3,2,1,0:T(8,128)(2,1)S(1)} copy-done((bf16[3,3,16,32]{3,2,1,0:T(8,128)(2,1)S(1)}, bf16[3,3,16,32]{3,2,1,0:T(8,128)(2,1)}, u32[]{:S(2)}) %copy-start.3) | copy-done | bytes 9240
  5.3 0.0 copy-start.4
  5.3 0.7 %copy-done.4 = s32[96]{0:T(128)S(1)} copy-done((s32[96]{0:T(128)S(1)}, s32[96]{0:T(128)}, u32[]{:S(2)}) %copy-start.4) | copy-done | bytes 408
  5.9 0.0 copy-start.5
  5.9 0.7 %copy-done.5 = s32[96]{0:T(128)S(1)} copy-done((s32[96]{0:T(128)S(1)}, s32[96]{0:T(128)}, u32[]{:S(2)}) %copy-start.5) | copy-done | bytes 408
  6.6 0.0 copy-start.6
  6.6 0.7 %copy-done.6 = s32[96]{0:T(128)S(1)} copy-done((s32[96]{0:T(128)S(1)}, s32[96]{0:T(128)}, u32[]{:S(2)}) %copy-start.6) | copy-done | bytes 408
  7.3 0.0 copy-start.7
  7.3 0.7 %copy-done.7 = s32[1,16]{1,0:T(1,128)S(1)} copy-done((s32[1,16]{1,0:T(1,128)S(1)}, s32[1,16]{1,0:T(1,128)}, u32[]{:S(2)}) %copy-start.7) | copy-done | bytes 88
  7.9 40.9 %shard_map.103 = (bf16[32,8,1024]{2,1,0:T(8,128)(2,1)S(1)}, f32[144,32]{1,0:T(8,128)S(1)}, f32[6,16,128]{2,1,0:T(8,128)S(1)}) custom-call(s32[96]{0:T(128)S(1)} %copy-done.4, s32[96]{0:T(128)S(1)} %copy-done.5, s32[96]{0:T(128)S(1)} %copy-done.6, s32[1,96]{1,0:T(1,128)S(1)} %bitcast.15, s32[1,96]{1,0:T(1,128)S(1)} %bitcast.16, s32[1,96]{1,0:T(1,128)S(1)} %bitcast.17, ...), custom_call_target="tpu_custom_call" | custom-call | tf_op jit(solution)/shard_map/pallas_call | solution.py:424
  48.8 0.8 %copy.14 = bf16[1,32,8,1024]{3,2,1,0:T(8,128)(2,1)} copy(bf16[1,32,8,1024]{3,2,1,0:T(8,128)(2,1)S(1)} %bitcast.10) | data formatting | bytes 1048576
  49.6 0.6 %copy.15 = f32[3,3,16,32]{3,2,1,0:T(8,128)} copy(f32[3,3,16,32]{3,2,1,0:T(8,128)S(1)} %bitcast.12) | data formatting | bytes 36864
  50.2 0.6 %copy.16 = f32[1,6,16,128]{3,2,1,0:T(8,128)} copy(f32[1,6,16,128]{3,2,1,0:T(8,128)S(1)} %bitcast.13) | data formatting | bytes 98304
Async XLA Ops:
  0.6 1.9 %copy-start = (bf16[96,128,128]{2,1,0:T(8,128)(2,1)S(1)}, bf16[96,128,128]{2,1,0:T(8,128)(2,1)}, u32[]{:S(2)}) copy-start(bf16[96,128,128]{2,1,0:T(8,128)(2,1)} %weights.1) | copy-start | bytes 9437188
  2.5 1.0 %copy-start.1 = (bf16[1,32,8,1024]{3,2,1,0:T(8,128)(2,1)S(1)}, bf16[1,32,8,1024]{3,2,1,0:T(8,128)(2,1)}, u32[]{:S(2)}) copy-start(bf16[1,32,8,1024]{3,2,1,0:T(8,128)(2,1)} %param.9) | copy-start | bytes 1572868
  3.6 0.9 %copy-start.2 = (bf16[1,16,8,1024]{3,2,1,0:T(8,128)(2,1)S(1)}, bf16[1,16,8,1024]{3,2,1,0:T(8,128)(2,1)}, u32[]{:S(2)}) copy-start(bf16[1,16,8,1024]{3,2,1,0:T(8,128)(2,1)} %param.8) | copy-start | bytes 786436
  4.5 0.8 %copy-start.3 = (bf16[3,3,16,32]{3,2,1,0:T(8,128)(2,1)S(1)}, bf16[3,3,16,32]{3,2,1,0:T(8,128)(2,1)}, u32[]{:S(2)}) copy-start(bf16[3,3,16,32]{3,2,1,0:T(8,128)(2,1)} %param.10) | copy-start | bytes 27652
  5.3 0.7 %copy-start.4 = (s32[96]{0:T(128)S(1)}, s32[96]{0:T(128)}, u32[]{:S(2)}) copy-start(s32[96]{0:T(128)} %ft_s.1) | copy-start | bytes 1156
  5.9 0.7 %copy-start.5 = (s32[96]{0:T(128)S(1)}, s32[96]{0:T(128)}, u32[]{:S(2)}) copy-start(s32[96]{0:T(128)} %ct_s.1) | copy-start | bytes 1156
  6.6 0.7 %copy-start.6 = (s32[96]{0:T(128)S(1)}, s32[96]{0:T(128)}, u32[]{:S(2)}) copy-start(s32[96]{0:T(128)} %os_s.1) | copy-start | bytes 1156
  7.3 0.7 %copy-start.7 = (s32[1,16]{1,0:T(1,128)S(1)}, s32[1,16]{1,0:T(1,128)}, u32[]{:S(2)}) copy-start(s32[1,16]{1,0:T(1,128)} %sc_v.1) | copy-start | bytes 196

commit v2 on v1

--- a/solution.py
+++ b/solution.py
@@ -22,17 +22,14 @@
 
 def kernel(
     dims,
-    ft_s,
-    ct_s,
-    os_s,
-    ft_v,
-    ct_v,
-    os_v,
-    sc_v,
-    go,
-    feat,
-    cw,
-    weights,
+    ft_h,
+    ct_h,
+    os_h,
+    sc_h,
+    go_h,
+    feat_h,
+    cw_h,
+    weights_h,
     gf_out,
     cg_out,
     co_out,
@@ -52,7 +49,22 @@
     halo,
     ar1,
     ar2,
-    ar3,
+    weights,
+    weights_t,
+    go,
+    feat,
+    cw,
+    ft_s,
+    ct_s,
+    os_s,
+    ft_v,
+    ct_v,
+    os_v,
+    sc_v,
+    loads,
+    wloads,
+    fhs,
+    fhr,
     s1s,
     s1r,
     s2s,
@@ -66,8 +78,6 @@
     a1r,
     a2s,
     a2r,
-    a3s,
-    a3r,
 ):
     n_dp, bands, n1, n2, channels, cin, rows, cols, tl, nb, per, ct_all, scaling = dims
     cblocks = cols // tl
@@ -89,12 +99,16 @@
     def greet(device):
         pl.semaphore_signal(barrier, inc=1, device_id=device, device_id_type=MESH)
 
-    for d in range(1, n1):
-        greet(inner((my_i + d) % n1))
+    plane_count = n1 * n_dp
+    my_p = my_dp * n1 + my_i
+
+    def plane(p):
+        return {"dp": p // n1, "band": my_o * n1 + p % n1}
+
+    for d in range(1, plane_count):
+        greet(plane((my_p + d) % plane_count))
     for e in range(1, n2):
         greet(outer((my_o + e) % n2))
-    for f in range(1, n_dp):
-        greet({"dp": (my_dp + f) % n_dp})
 
     @pl.when(me > 0)
     def _():
@@ -103,6 +117,35 @@
     @pl.when(me < bands - 1)
     def _():
         greet({"band": me + 1})
+
+    ins = []
+    for n, (src, dst) in enumerate(
+        [
+            (go_h, go),
+            (ft_h, ft_s),
+            (ct_h, ct_s),
+            (os_h, os_s),
+            (ft_h, ft_v),
+            (ct_h, ct_v),
+            (os_h, os_v),
+            (sc_h, sc_v),
+            (feat_h, feat),
+            (cw_h, cw),
+        ]
+    ):
+        ins.append(pltpu.make_async_copy(src, dst, loads.at[n]))
+    w_chunks = wloads.shape[0]
+    w_len = nb // w_chunks
+    w_ins = [
+        pltpu.make_async_copy(
+            weights_h.at[pl.ds(n * w_len, w_len)], weights.at[pl.ds(n * w_len, w_len)], wloads.at[n]
+        )
+        for n in range(w_chunks)
+    ]
+    for copy in ins[:8] + w_ins + ins[8:]:
+        copy.start()
+    for copy in ins[:8]:
+        copy.wait()
 
     for b in range(cblocks):
         part = go[:, :, b * tl : (b + 1) * tl].astype(F32)
@@ -116,11 +159,13 @@
     def forward(t, carry):
         for a in range(step):
             k = t * step + a
-            product = jnp.dot(tiles[ft_s[k]], weights[k], preferred_element_type=F32)
+            product = jnp.dot(tiles[ft_s[0, k]], weights[k], preferred_element_type=F32)
             terms[pl.ds(pl.multiple_of(k * channels, channels), channels), :] = product
         return carry
 
-    lax.fori_loop(0, nb // step, forward, 0)
+    for n in range(w_chunks):
+        w_ins[n].wait()
+        lax.fori_loop(n * w_len // step, (n + 1) * w_len // step, forward, 0)
 
     def owner_parts(slot):
         owner = lax.shift_right_logical(slot * (65536 // per + 1), 16)
@@ -141,9 +186,6 @@
     row_of_block = jnp.where(in_use, row_of_block, -1)
     select = (lax.broadcasted_iota(jnp.int32, (ct_all, nb), 0) == row_of_block).astype(F32)
     select = jnp.concatenate([select.astype(BF16)] * 2, axis=1)
-    fine = jnp.where(in_use, ft_v[...], -1)
-    pick = (lax.broadcasted_iota(jnp.int32, (n_tiles, nb), 0) == fine).astype(F32)
-    pick = jnp.concatenate([pick.astype(BF16)] * 2, axis=1)
 
     def gather_sum(chooser, target, count):
         for c in range(0, channels, 2):
@@ -157,7 +199,7 @@
     gather_sum(select, sums, ct_all)
     tx1[...] = sums[...].astype(BF16).reshape(ct_all, channels, tl)
 
-    peers = (n1 - 1) + (n2 - 1) + (n_dp - 1)
+    peers = (plane_count - 1) + (n2 - 1)
     peers = peers + jnp.minimum(me, 1) + jnp.minimum(bands - 1 - me, 1)
     pl.semaphore_wait(barrier, peers)
 
@@ -172,43 +214,83 @@
         )
 
     first = []
-    for d in range(1, n1):
-        to = (my_i + d) % n1
-        copy = remote(
-            tx1.at[pl.ds(to * group, group)], rx1.at[d - 1], s1s.at[d - 1], s1r.at[d - 1], inner(to)
-        )
-        copy.start()
-        first.append(copy)
-
+    for e in range(1, n2 + 1):
+        z = (my_o + e) % n2
+        for d in range(1, n1):
+            to = (my_i + d) % n1
+            copy = remote(
+                tx1.at[pl.ds((to * n2 + z) * per, per)],
+                rx1.at[d - 1, e - 1],
+                s1s.at[d - 1, e - 1],
+                s1r.at[d - 1, e - 1],
+                inner(to),
+            )
+            copy.start()
+            first.append(copy)
+
+    def transpose_weights(lo, hi):
+        def body(k, carry):
+            weights_t[k] = weights[k].T
+            return carry
+
+        lax.fori_loop(lo, hi, body, 0)
+
+    ins[8].wait()
+    ins[9].wait()
     for b in range(cblocks):
         part = feat[:, :, b * tl : (b + 1) * tl].astype(F32)
         stage[b] = part.reshape(cin * rows, tl)
         for r in range(rows):
             line = stage[b, pl.ds(r, cin, stride=rows), :]
-            featr[r, :, b * tl : (b + 1) * tl] = line.astype(BF16)
+            featr[r + 1, :, b * tl : (b + 1) * tl] = line.astype(BF16)
+
+    up_dev = {"band": jnp.maximum(me - 1, 0)}
+    down_dev = {"band": jnp.minimum(me + 1, bands - 1)}
+    f_up = remote(featr.at[1], featr.at[rows + 1], fhs.at[0], fhr.at[1], up_dev)
+    f_down = remote(featr.at[rows], featr.at[0], fhs.at[1], fhr.at[0], down_dev)
+
+    @pl.when(me > 0)
+    def _():
+        f_up.start()
+
+    @pl.when(me == 0)
+    def _():
+        featr[0] = jnp.zeros((cin, cols), BF16)
+
+    @pl.when(me < bands - 1)
+    def _():
+        f_down.start()
+
+    @pl.when(me == bands - 1)
+    def _():
+        featr[rows + 1] = jnp.zeros((cin, cols), BF16)
+
+    fine = jnp.where(in_use, ft_v[...], -1)
+    pick = (lax.broadcasted_iota(jnp.int32, (n_tiles, nb), 0) == fine).astype(F32)
+    pick = jnp.concatenate([pick.astype(BF16)] * 2, axis=1)
     slab = 3 * channels
     kernel_rows = jnp.concatenate([cw[(2 - p) * slab : (3 - p) * slab, :] for p in range(3)], axis=0)
     kernel_t = kernel_rows.astype(F32).T.astype(BF16)
 
-    for copy in first:
-        copy.wait()
-
     size = per * channels
 
-    def inner_sum(z):
+    def inner_sum(z, e):
+        for copy in first[(e - 1) * (n1 - 1) : e * (n1 - 1)]:
+            copy.wait()
         own = sums[pl.ds(pl.multiple_of((my_i * group + z * per) * channels, size), size), :]
         for d in range(n1 - 1):
-            own = own + rx1[d, pl.ds(z * per, per)].astype(F32).reshape(size, tl)
+            own = own + rx1[d, e - 1].astype(F32).reshape(size, tl)
         return own
 
     second = []
     for e in range(1, n2):
         to = (my_o + e) % n2
-        tx2[e - 1] = inner_sum(to).astype(BF16).reshape(per, channels, tl)
+        tx2[e - 1] = inner_sum(to, e).astype(BF16).reshape(per, channels, tl)
         copy = remote(tx2.at[e - 1], rx2.at[e - 1], s2s.at[e - 1], s2r.at[e - 1], outer(to))
         copy.start()
         second.append(copy)
-    owned = inner_sum(my_o)
+    owned = inner_sum(my_o, n2)
+    transpose_weights(0, nb // 2)
     for e in range(1, n2):
         second[e - 1].wait()
         owned = owned + rx2[e - 1].astype(F32).reshape(size, tl)
@@ -236,6 +318,7 @@
         sent.append(copy)
     pass_on(my_o, 0)
     co_out[...] = owned.reshape(per, channels, tl)
+    transpose_weights(nb // 2, nb)
     for e in range(1, n2):
         z = (my_o + n2 - e) % n2
         here = place(my_i, z)
@@ -257,8 +340,8 @@
     def backward(t, carry):
         for a in range(step):
             k = t * step + a
-            value = back[row_index(os_s[ct_s[k]])]
-            product = lax.dot_general(value, weights[k], NT, preferred_element_type=F32)
+            value = back[row_index(os_s[0, ct_s[0, k]])]
+            product = jnp.dot(value, weights_t[k], preferred_element_type=F32)
             terms[pl.ds(pl.multiple_of(k * channels, channels), channels), :] = product
         return carry
 
@@ -285,10 +368,8 @@
     top, bottom = mid_row(0), mid_row(rows - 1)
     edges[0] = top
     edges[1] = bottom
-    up = remote(edges.at[0], halo.at[1], hs.at[0], hr.at[1], {"band": jnp.maximum(me - 1, 0)})
-    down = remote(
-        edges.at[1], halo.at[0], hs.at[1], hr.at[0], {"band": jnp.minimum(me + 1, bands - 1)}
-    )
+    up = remote(edges.at[0], halo.at[1], hs.at[0], hr.at[1], up_dev)
+    down = remote(edges.at[1], halo.at[0], hs.at[1], hr.at[0], down_dev)
 
     @pl.when(me > 0)
     def _():
@@ -303,43 +384,26 @@
     for r in range(1, rows - 1):
         put_row(r + 1, mid_row(r))
 
-    def conv_row(r, total):
-        window = comb[r * slab : (r + 3) * slab, :]
-        result = jnp.dot(kernel_t, window, preferred_element_type=F32)
-        for b in range(cblocks):
-            stage[b, pl.ds(r, cin, stride=rows), :] = result[:, b * tl : (b + 1) * tl]
-        return total + lax.dot_general(window, featr[r], NT, preferred_element_type=F32)
-
-    total = jnp.zeros((3 * slab, cin), F32)
-    for r in range(1, rows - 1):
-        total = conv_row(r, total)
-
     @pl.when(me > 0)
     def _():
-        down.wait_recv()
-        put_row(0, halo[0])
-
-    @pl.when(me == 0)
-    def _():
-        comb[0:slab, :] = jnp.zeros((slab, cols), BF16)
+        f_down.wait_recv()
+        f_up.wait_send()
 
     @pl.when(me < bands - 1)
     def _():
-        up.wait_recv()
-        put_row(rows + 1, halo[1])
-
-    @pl.when(me == bands - 1)
-    def _():
-        comb[(rows + 1) * slab : (rows + 2) * slab, :] = jnp.zeros((slab, cols), BF16)
-
-    total = conv_row(0, total)
-    total = conv_row(rows - 1, total)
-
+        f_up.wait_recv()
+        f_down.wait_send()
+
+    total = jnp.zeros((slab, 3 * cin), F32)
+    for r in range(rows):
+        near = featr[r : r + 3].reshape(3 * cin, cols)
+        line = comb[(r + 1) * slab : (r + 2) * slab, :]
+        total = total + lax.dot_general(line, near, NT, preferred_element_type=F32)
     total = total * scaling
-    packs = 128 // cin
     lines = ar1.shape[1]
-    full = jnp.concatenate([total, jnp.zeros((packs * lines - 3 * slab, cin), F32)], axis=0)
-    packed = jnp.concatenate([full[a * lines : (a + 1) * lines] for a in range(packs)], axis=1)
+    extra = [total[lines:, u * cin : (u + 1) * cin] for u in range(3)]
+    extra.append(jnp.zeros((lines - 3 * (slab - lines), cin), F32))
+    packed = jnp.concatenate([total[:lines], jnp.concatenate(extra, axis=0)], axis=1)
 
     def exchange(value, buf, send, recv, count, index, device):
         buf[index] = value
@@ -370,18 +434,47 @@
 
         return finish
 
-    finish = exchange(packed, ar1, a1s, a1r, n1, my_i, inner)
+    finish = exchange(packed, ar1, a1s, a1r, plane_count, my_p, plane)
+
+    def conv_row(r):
+        window = comb[r * slab : (r + 3) * slab, :]
+        result = jnp.dot(kernel_t, window, preferred_element_type=F32)
+        for b in range(cblocks):
+            stage[b, pl.ds(r, cin, stride=rows), :] = result[:, b * tl : (b + 1) * tl]
+
+    for r in range(1, rows - 1):
+        conv_row(r)
+
+    finish = exchange(finish(), ar2, a2s, a2r, n2, my_o, outer)
+
+    @pl.when(me > 0)
+    def _():
+        down.wait_recv()
+        put_row(0, halo[0])
+
+    @pl.when(me == 0)
+    def _():
+        comb[0:slab, :] = jnp.zeros((slab, cols), BF16)
+
+    @pl.when(me < bands - 1)
+    def _():
+        up.wait_recv()
+        put_row(rows + 1, halo[1])
+
+    @pl.when(me == bands - 1)
+    def _():
+        comb[(rows + 1) * slab : (rows + 2) * slab, :] = jnp.zeros((slab, cols), BF16)
+
+    conv_row(0)
+    conv_row(rows - 1)
     for b in range(cblocks):
         part = stage[b].reshape(cin, rows, tl)
         gf_out[:, :, b * tl : (b + 1) * tl] = part.astype(BF16)
     packed = finish()
-    packed = exchange(packed, ar2, a2s, a2r, n2, my_o, outer)()
-    packed = exchange(packed, ar3, a3s, a3r, n_dp, my_dp, lambda y: {"dp": y})()
+    rest = slab - lines
     for u in range(3):
-        for s in range((2 - u) * slab, (3 - u) * slab, 8):
-            a, b = s // lines, s % lines
-            at = u * slab + s - (2 - u) * slab
-            cg_out[at : at + 8, :] = packed[b : b + 8, a * cin : (a + 1) * cin]
+        cg_out[u * slab : u * slab + lines, :] = packed[:, u * cin : (u + 1) * cin]
+        cg_out[u * slab + lines : (u + 1) * slab, :] = packed[u * rest : (u + 1) * rest, 3 * cin :]
 
     @pl.when(me > 0)
     def _():
@@ -390,6 +483,15 @@
     @pl.when(me < bands - 1)
     def _():
         down.wait_send()
+
+
+def write_out(gf_in, cg_in, co_in, gf_out, cg_out, co_out, sems):
+    pairs = ((gf_in, gf_out), (cg_in, cg_out), (co_in, co_out))
+    copies = [pltpu.make_async_copy(a, b, sems.at[n]) for n, (a, b) in enumerate(pairs)]
+    for copy in copies:
+        copy.start()
+    for copy in copies:
+        copy.wait()
 
 
 def per_device(
@@ -415,12 +517,10 @@
     scaling = 1.0 / math.sqrt(n_dp * bands * rows * cols)
     dims = (n_dp, bands, n1, n2, channels, cin, rows, cols, tl, nb, per, ct_all, scaling)
     slab = 3 * channels
-    packs = 128 // cin
-    lines = -(-3 * slab // (packs * 8)) * 8
-    group = n2 * per
+    lines = slab - 8
+    w_chunks = 4
     dma = pltpu.SemaphoreType.DMA
     vmem = pl.BlockSpec(memory_space=pltpu.VMEM)
-    smem = pl.BlockSpec(memory_space=pltpu.SMEM)
     gf, cg, co = pl.pallas_call(
         functools.partial(kernel, dims),
         out_shape=(
@@ -428,7 +528,7 @@
             jax.ShapeDtypeStruct((3 * slab, cin), F32),
             jax.ShapeDtypeStruct((per, channels, tl), F32),
         ),
-        in_specs=[smem] * 3 + [vmem] * 8,
+        in_specs=[pl.BlockSpec(memory_space=pltpu.HBM)] * 8,
         out_specs=(vmem, vmem, vmem),
         scratch_shapes=[
             pltpu.VMEM((cols // tl, cin * rows, tl), F32),
@@ -436,20 +536,35 @@
             pltpu.VMEM((nb * channels, tl), F32),
             pltpu.VMEM((ct_all * channels, tl), F32),
             pltpu.VMEM((ct_all, channels, tl), BF16),
-            pltpu.VMEM((n1 - 1, group, channels, tl), BF16),
+            pltpu.VMEM((n1 - 1, n2, per, channels, tl), BF16),
             pltpu.VMEM((n2 - 1, per, channels, tl), BF16),
             pltpu.VMEM((n2 - 1, per, channels, tl), BF16),
             pltpu.VMEM((ct_all, channels, tl), BF16),
             pltpu.VMEM((n_tiles * channels, tl), F32),
             pltpu.VMEM(((rows + 2) * slab, cols), BF16),
-            pltpu.VMEM((rows, cin, cols), BF16),
+            pltpu.VMEM((rows + 2, cin, cols), BF16),
             pltpu.VMEM((2, channels, cols), BF16),
             pltpu.VMEM((2, channels, cols), BF16),
-            pltpu.VMEM((n1, lines, 128), F32),
-            pltpu.VMEM((n2, lines, 128), F32),
-            pltpu.VMEM((n_dp, lines, 128), F32),
-            dma((n1 - 1,)),
-            dma((n1 - 1,)),
+            pltpu.VMEM((n1 * n_dp, lines, 4 * cin), F32),
+            pltpu.VMEM((n2, lines, 4 * cin), F32),
+            pltpu.VMEM((nb, tl, tl), BF16),
+            pltpu.VMEM((nb, tl, tl), BF16),
+            pltpu.VMEM((channels, rows, cols), BF16),
+            pltpu.VMEM((cin, rows, cols), BF16),
+            pltpu.VMEM((3 * slab, cin), BF16),
+            pltpu.SMEM((1, nb), jnp.int32),
+            pltpu.SMEM((1, nb), jnp.int32),
+            pltpu.SMEM((1, ct_all), jnp.int32),
+            pltpu.VMEM((1, nb), jnp.int32),
+            pltpu.VMEM((1, nb), jnp.int32),
+            pltpu.VMEM((1, ct_all), jnp.int32),
+            pltpu.VMEM((1, bands), jnp.int32),
+            dma((10,)),
+            dma((w_chunks,)),
+            dma((2,)),
+            dma((2,)),
+            dma((n1 - 1, n2)),
+            dma((n1 - 1, n2)),
             dma((n2 - 1,)),
             dma((n2 - 1,)),
             dma((n2 - 1,)),
@@ -457,20 +572,15 @@
             dma((n1, n2)),
             dma((2,)),
             dma((2,)),
-            dma((n1 - 1,)),
-            dma((n1,)),
+            dma((n1 * n_dp - 1,)),
+            dma((n1 * n_dp,)),
             dma((n2 - 1,)),
             dma((n2,)),
-            dma((n_dp - 1,)),
-            dma((n_dp,)),
         ],
         compiler_params=pltpu.CompilerParams(
-            collective_id=0, has_side_effects=True, vmem_limit_bytes=48 * 1024 * 1024
+            collective_id=0, has_side_effects=True, vmem_limit_bytes=64 * 1024 * 1024
         ),
     )(
-        fine_tile,
-        coarse_tile,
-        owner_slot,
         fine_tile.reshape(1, nb),
         coarse_tile.reshape(1, nb),
         owner_slot.reshape(1, ct_all),
@@ -480,6 +590,14 @@
         conv_weight.reshape(3 * slab, cin),
         block_weights,
     )
+    hbm = pl.BlockSpec(memory_space=pltpu.HBM)
+    gf, cg, co = pl.pallas_call(
+        write_out,
+        out_shape=tuple(jax.ShapeDtypeStruct(x.shape, x.dtype) for x in (gf, cg, co)),
+        in_specs=[pl.BlockSpec(memory_space=pl.ANY)] * 3,
+        out_specs=(hbm,) * 3,
+        scratch_shapes=[dma((3,))],
+    )(gf, cg, co)
     return gf[None], cg.reshape(3, 3, channels, cin), co[None]
 
 

time: 51.2 us -> 61.8 us (1.21)
  Pallas kernels: 40.9 us -> 61 us
  local copies, waits for them, and re-layouts: 9.31 us -> 0 us
    pallas_call x0 -> x1, Pallas kernels: none -> 20.7 us  [per_device(): pl.pallas_call(write_out, out_shape=tuple((jax.ShapeDtypeStruct(x.shape,...]
    unnamed x19 -> x0, local copies, waits for them, and re-layouts: 9.31 us -> none
    pallas_call x1, Pallas kernels: 40.9 us -> 40.2 us  [per_device(): pl.pallas_call(functools.partial(kernel, dims), out_shape=(jax.ShapeDtype...]
where the time goes in v2:
time: 61.8 us; the launch traced here: 61.6 us
  Pallas kernels  61 us (99%)
  between operations  0.64 us (1%)
    pallas_call x1, Pallas kernels, per_device(): pl.pallas_call(functools.partial(kernel, dims), out_shape=(jax.ShapeDtype...  40.2 us
    pallas_call x1, Pallas kernels, per_device(): pl.pallas_call(write_out, out_shape=tuple((jax.ShapeDtypeStruct(x.shape,...  20.7 us

profile of v2, /device:TPU:0, one launch (start us, length us, event | category | flops | bytes accessed | tf_op | source)
XLA Modules:
  0.0 61.6 jit_solution(10486408899537091807)
XLA Ops:
  0.6 40.2 %shard_map.103 = (bf16[32,8,1024]{2,1,0:T(8,128)(2,1)}, f32[144,32]{1,0:T(8,128)}, f32[6,16,128]{2,1,0:T(8,128)}) custom-call(s32[1,96]{1,0:T(1,128)} %bitcast.12, s32[1,96]{1,0:T(1,128)} %bitcast.13, s32[1,96]{1,0:T(1,128)} %bitcast.14, s32[1,16]{1,0:T(1,128)} %sc_h.1, bf16[16,8,1024]{2,1,0:T(8,128)(2,1)} %bitcast.10, bf16[32,8,1024]{2,1,0:T(8,128)(2,1)} %bitcast.9, ...), custom_call_target="tpu_custom_call" | custom-call | tf_op jit(solution)/shard_map/pallas_call | solution.py:524
  40.9 20.7 %shard_map.104 = (bf16[32,8,1024]{2,1,0:T(8,128)(2,1)}, f32[144,32]{1,0:T(8,128)}, f32[6,16,128]{2,1,0:T(8,128)}) custom-call(bf16[32,8,1024]{2,1,0:T(8,128)(2,1)} %get-tuple-element.9.gf_in, f32[144,32]{1,0:T(8,128)} %get-tuple-element.10.cg_in, f32[6,16,128]{2,1,0:T(8,128)} %get-tuple-element.11.co_in), custom_call_target="tpu_custom_call" | custom-call | tf_op jit(solution)/shard_map/pallas_call | solution.py:594

commit v3 on v2

--- a/solution.py
+++ b/solution.py
@@ -47,10 +47,11 @@
     featr,
     edges,
     halo,
+    ar0,
     ar1,
     ar2,
+    ar3,
     weights,
-    weights_t,
     go,
     feat,
     cw,
@@ -78,6 +79,8 @@
     a1r,
     a2s,
     a2r,
+    a3s,
+    a3r,
 ):
     n_dp, bands, n1, n2, channels, cin, rows, cols, tl, nb, per, ct_all, scaling = dims
     cblocks = cols // tl
@@ -228,13 +231,6 @@
             copy.start()
             first.append(copy)
 
-    def transpose_weights(lo, hi):
-        def body(k, carry):
-            weights_t[k] = weights[k].T
-            return carry
-
-        lax.fori_loop(lo, hi, body, 0)
-
     ins[8].wait()
     ins[9].wait()
     for b in range(cblocks):
@@ -290,7 +286,6 @@
         copy.start()
         second.append(copy)
     owned = inner_sum(my_o, n2)
-    transpose_weights(0, nb // 2)
     for e in range(1, n2):
         second[e - 1].wait()
         owned = owned + rx2[e - 1].astype(F32).reshape(size, tl)
@@ -302,34 +297,44 @@
 
     sent = []
 
-    def pass_on(z, e):
-        here = place(my_i, z)
-        for d in range(1, n1):
-            copy = remote(
-                here, here, gis.at[d - 1, e], grs.at[my_i, z], inner((my_i + d) % n1)
-            )
-            copy.start()
-            sent.append(copy)
-
-    mine = place(my_i, my_o)
-    for e in range(1, n2):
-        copy = remote(mine, mine, gos.at[e - 1], grs.at[my_i, my_o], outer((my_o + e) % n2))
+    side = my_i + 1 - 2 * (my_i % 2)
+    across = (my_i + 2) % n1
+    corner = (side + 2) % n1
+
+    def hand(i, z, send, device):
+        here = place(i, z)
+        copy = remote(here, here, send, grs.at[i, z], device)
         copy.start()
         sent.append(copy)
+
+    def take(i, z, send, device):
+        here = place(i, z)
+        remote(here, here, send, grs.at[i, z], device).wait_recv()
+
+    def pass_on(z, e):
+        hand(my_i, z, gis.at[0, e], inner(across))
+        hand(my_i, z, gis.at[1, e], inner(side))
+
+    for e in range(1, n2):
+        hand(my_i, my_o, gos.at[e - 1], outer((my_o + e) % n2))
     pass_on(my_o, 0)
     co_out[...] = owned.reshape(per, channels, tl)
-    transpose_weights(nb // 2, nb)
-    for e in range(1, n2):
+    for e in range(n2):
         z = (my_o + n2 - e) % n2
-        here = place(my_i, z)
-        remote(here, here, gos.at[e - 1], grs.at[my_i, z], outer(z)).wait_recv()
-        pass_on(z, e)
-    for d in range(1, n1):
-        i = (my_i + d) % n1
-        for e in range(n2):
-            z = (my_o + n2 - e) % n2
-            here = place(i, z)
-            remote(here, here, gis.at[d - 1, e], grs.at[i, z], inner(i)).wait_recv()
+        if e > 0:
+            take(my_i, z, gos.at[e - 1], outer(z))
+            pass_on(z, e)
+        if e > 0:
+            zp = (my_o + n2 - e + 1) % n2
+            take(across, zp, gis.at[0, e - 1], inner(across))
+            hand(across, zp, gis.at[2, e - 1], inner(side))
+    zp = (my_o + 1) % n2
+    take(across, zp, gis.at[0, n2 - 1], inner(across))
+    hand(across, zp, gis.at[2, n2 - 1], inner(side))
+    for e in range(n2):
+        z = (my_o + n2 - e) % n2
+        take(side, z, gis.at[1, e], inner(side))
+        take(corner, z, gis.at[2, e], inner(side))
     for copy in sent:
         copy.wait_send()
 
@@ -341,7 +346,7 @@
         for a in range(step):
             k = t * step + a
             value = back[row_index(os_s[0, ct_s[0, k]])]
-            product = jnp.dot(value, weights_t[k], preferred_element_type=F32)
+            product = lax.dot_general(value, weights[k], NT, preferred_element_type=F32)
             terms[pl.ds(pl.multiple_of(k * channels, channels), channels), :] = product
         return carry
 
@@ -400,12 +405,18 @@
         line = comb[(r + 1) * slab : (r + 2) * slab, :]
         total = total + lax.dot_general(line, near, NT, preferred_element_type=F32)
     total = total * scaling
-    lines = ar1.shape[1]
-    extra = [total[lines:, u * cin : (u + 1) * cin] for u in range(3)]
-    extra.append(jnp.zeros((lines - 3 * (slab - lines), cin), F32))
-    packed = jnp.concatenate([total[:lines], jnp.concatenate(extra, axis=0)], axis=1)
-
-    def exchange(value, buf, send, recv, count, index, device):
+    total = jnp.concatenate([total, jnp.zeros((slab, cin), F32)], axis=1)
+    ar0[...] = jnp.zeros(ar0.shape, F32)
+    ar0[0 : slab // 8] = total.reshape(slab // 8, 8, 4 * cin)
+    ar1[my_p] = ar0[my_p]
+    scatter = []
+    for d in range(1, plane_count):
+        to = (my_p + d) % plane_count
+        copy = remote(ar0.at[to], ar1.at[my_p], a1s.at[d - 1], a1r.at[my_p], plane(to))
+        copy.start()
+        scatter.append(copy)
+
+    def exchange(value, buf, send, recv, count, index, device, summed):
         buf[index] = value
         copies = []
         for d in range(1, count):
@@ -427,14 +438,14 @@
                 ).wait_recv()
             for copy in copies:
                 copy.wait_send()
+            if not summed:
+                return None
             result = buf[0]
             for m in range(1, count):
                 result = result + buf[m]
             return result
 
         return finish
-
-    finish = exchange(packed, ar1, a1s, a1r, plane_count, my_p, plane)
 
     def conv_row(r):
         window = comb[r * slab : (r + 3) * slab, :]
@@ -442,10 +453,25 @@
         for b in range(cblocks):
             stage[b, pl.ds(r, cin, stride=rows), :] = result[:, b * tl : (b + 1) * tl]
 
-    for r in range(1, rows - 1):
+    half = rows // 2
+    for r in range(1, half):
         conv_row(r)
 
-    finish = exchange(finish(), ar2, a2s, a2r, n2, my_o, outer)
+    for d in range(1, plane_count):
+        source = (my_p + d) % plane_count
+        remote(
+            ar0.at[source], ar1.at[source], a1s.at[d - 1], a1r.at[source], plane(source)
+        ).wait_recv()
+    for copy in scatter:
+        copy.wait_send()
+    share = ar1[0]
+    for m in range(1, plane_count):
+        share = share + ar1[m]
+    finish = exchange(share, ar2, a2s, a2r, n2, my_o, outer, True)
+    for r in range(half, rows - 1):
+        conv_row(r)
+
+    finish = exchange(finish(), ar3, a3s, a3r, plane_count, my_p, plane, False)
 
     @pl.when(me > 0)
     def _():
@@ -470,11 +496,10 @@
     for b in range(cblocks):
         part = stage[b].reshape(cin, rows, tl)
         gf_out[:, :, b * tl : (b + 1) * tl] = part.astype(BF16)
-    packed = finish()
-    rest = slab - lines
+    finish()
+    total = ar3[0 : slab // 8].reshape(slab, 4 * cin)
     for u in range(3):
-        cg_out[u * slab : u * slab + lines, :] = packed[:, u * cin : (u + 1) * cin]
-        cg_out[u * slab + lines : (u + 1) * slab, :] = packed[u * rest : (u + 1) * rest, 3 * cin :]
+        cg_out[u * slab : (u + 1) * slab, :] = total[:, u * cin : (u + 1) * cin]
 
     @pl.when(me > 0)
     def _():
@@ -485,13 +510,10 @@
         down.wait_send()
 
 
-def write_out(gf_in, cg_in, co_in, gf_out, cg_out, co_out, sems):
-    pairs = ((gf_in, gf_out), (cg_in, cg_out), (co_in, co_out))
-    copies = [pltpu.make_async_copy(a, b, sems.at[n]) for n, (a, b) in enumerate(pairs)]
-    for copy in copies:
-        copy.start()
-    for copy in copies:
-        copy.wait()
+def write_out(gf_in, cg_in, co_in, gf_out, cg_out, co_out):
+    gf_out[...] = gf_in[...]
+    cg_out[...] = cg_in[...]
+    co_out[...] = co_in[...]
 
 
 def per_device(
@@ -517,7 +539,7 @@
     scaling = 1.0 / math.sqrt(n_dp * bands * rows * cols)
     dims = (n_dp, bands, n1, n2, channels, cin, rows, cols, tl, nb, per, ct_all, scaling)
     slab = 3 * channels
-    lines = slab - 8
+    members = n1 * n_dp
     w_chunks = 4
     dma = pltpu.SemaphoreType.DMA
     vmem = pl.BlockSpec(memory_space=pltpu.VMEM)
@@ -545,9 +567,10 @@
             pltpu.VMEM((rows + 2, cin, cols), BF16),
             pltpu.VMEM((2, channels, cols), BF16),
             pltpu.VMEM((2, channels, cols), BF16),
-            pltpu.VMEM((n1 * n_dp, lines, 4 * cin), F32),
-            pltpu.VMEM((n2, lines, 4 * cin), F32),
-            pltpu.VMEM((nb, tl, tl), BF16),
+            pltpu.VMEM((members, 8, 4 * cin), F32),
+            pltpu.VMEM((members, 8, 4 * cin), F32),
+            pltpu.VMEM((n2, 8, 4 * cin), F32),
+            pltpu.VMEM((members, 8, 4 * cin), F32),
             pltpu.VMEM((nb, tl, tl), BF16),
             pltpu.VMEM((channels, rows, cols), BF16),
             pltpu.VMEM((cin, rows, cols), BF16),
@@ -576,6 +599,8 @@
             dma((n1 * n_dp,)),
             dma((n2 - 1,)),
             dma((n2,)),
+            dma((members - 1,)),
+            dma((members,)),
         ],
         compiler_params=pltpu.CompilerParams(
             collective_id=0, has_side_effects=True, vmem_limit_bytes=64 * 1024 * 1024
@@ -590,13 +615,11 @@
         conv_weight.reshape(3 * slab, cin),
         block_weights,
     )
-    hbm = pl.BlockSpec(memory_space=pltpu.HBM)
     gf, cg, co = pl.pallas_call(
         write_out,
         out_shape=tuple(jax.ShapeDtypeStruct(x.shape, x.dtype) for x in (gf, cg, co)),
-        in_specs=[pl.BlockSpec(memory_space=pl.ANY)] * 3,
-        out_specs=(hbm,) * 3,
-        scratch_shapes=[dma((3,))],
+        in_specs=[vmem] * 3,
+        out_specs=(vmem,) * 3,
     )(gf, cg, co)
     return gf[None], cg.reshape(3, 3, channels, cin), co[None]
 

time: 61.8 us -> 44.9 us (0.73)
  Pallas kernels: 61 us -> 44.2 us
    pallas_call x1, Pallas kernels: 20.7 us -> 1.92 us  [per_device(): pl.pallas_call(write_out, out_shape=tuple((jax.ShapeDtypeStruct(x.shape,...]
    pallas_call x1, Pallas kernels: 40.2 us -> 42.2 us  [per_device(): pl.pallas_call(functools.partial(kernel, dims), out_shape=(jax.ShapeDtype...]
where the time goes in v3:
time: 44.9 us; the launch traced here: 44.8 us
  Pallas kernels  44.2 us (98%)
  between operations  0.64 us (1%)
    pallas_call x1, Pallas kernels, per_device(): pl.pallas_call(functools.partial(kernel, dims), out_shape=(jax.ShapeDtype...  42.2 us
    pallas_call x1, Pallas kernels, per_device(): pl.pallas_call(write_out, out_shape=tuple((jax.ShapeDtypeStruct(x.shape,...  1.92 us

profile of v3, /device:TPU:0, one launch (start us, length us, event | category | flops | bytes accessed | tf_op | source)
XLA Modules:
  0.0 44.8 jit_solution(2512588409959028304)
XLA Ops:
  0.6 42.2 %shard_map.103 = (bf16[32,8,1024]{2,1,0:T(8,128)(2,1)}, f32[144,32]{1,0:T(8,128)}, f32[6,16,128]{2,1,0:T(8,128)}) custom-call(s32[1,96]{1,0:T(1,128)} %bitcast.12, s32[1,96]{1,0:T(1,128)} %bitcast.13, s32[1,96]{1,0:T(1,128)} %bitcast.14, s32[1,16]{1,0:T(1,128)} %sc_h.1, bf16[16,8,1024]{2,1,0:T(8,128)(2,1)} %bitcast.10, bf16[32,8,1024]{2,1,0:T(8,128)(2,1)} %bitcast.9, ...), custom_call_target="tpu_custom_call" | custom-call | tf_op jit(solution)/shard_map/pallas_call | solution.py:546
  42.9 1.9 %shard_map.104 = (bf16[32,8,1024]{2,1,0:T(8,128)(2,1)}, f32[144,32]{1,0:T(8,128)}, f32[6,16,128]{2,1,0:T(8,128)}) custom-call(bf16[32,8,1024]{2,1,0:T(8,128)(2,1)} %get-tuple-element.9.gf_in, f32[144,32]{1,0:T(8,128)} %get-tuple-element.10.cg_in, f32[6,16,128]{2,1,0:T(8,128)} %get-tuple-element.11.co_in), custom_call_target="tpu_custom_call" | custom-call | tf_op jit(solution)/shard_map/pallas_call | solution.py:618
